TPU v7x, 32 devices: a whole 2x2x4 slice. The times are simulated.
32 devices in a mesh: groups: 2 (over y), dp: 4 (over z), chan: 2 (over x), sub: 2 (over core).
Axes of the slice: x: 2, y: 2, z: 4, core: 2. Of those that a mesh axis runs over, the one named last changes fastest.
Arguments:
- features: bfloat16 [192, 128, 1536], P(('groups', 'dp', 'sub'), None, 'chan'), parts along dimension 0, may hold values from -6 to 6
- cotangent: bfloat16 [192, 128, 1536], P(('groups', 'dp', 'sub'), None, 'chan'), parts along dimension 0, may hold values from -0.076171875 to 0.076171875
- snake_alpha: float32 [1536], P('chan'), may hold values from 0.5 to 4
- conv_weight: bfloat16 [1536, 3, 1536], P('dp', None, 'chan'), may hold values from -0.09375 to 0.09375
- lengths: int32 [192], P(('groups', 'dp', 'sub')), parts along dimension 0, may hold values from 1 to 128, as said below
- kept_rows: int32 [16], P(('groups', 'dp', 'sub')), parts along dimension 0, may hold values from 1 to 6, as said below
- sent_rows: int32 [16], P(('groups', 'dp', 'sub')), parts along dimension 0, may hold values from 0 to 6, as said below
Outputs:
- balanced_out: bfloat16 [112, 128, 1536], P(('groups', 'dp', 'sub'), None, 'chan'), parts along dimension 0
- weight_grad: float32 [3072, 3, 1536], P(('groups', 'dp'), None, 'chan'), parts along dimension 0
There are 2 independent parts, one for each index of `groups`. A program takes and returns all parts, laid end to end along the dimension named above; an argument that names none is the same for every part. Nothing has to cross between parts.
Inputs may be any that keep to these rules, and one draw needn't show every extreme that they name: `kept_rows`: each device keeps at least one row; one device keeps 6. kept_rows[h] + sent_rows[p] <= 7 for every device h and its previous device p; some device hands on 6 rows and some none. The first slot of every device has length 128; lengths of empty slots are not read.
All inputs are finite; a program needn't handle non-finite values.
Results may differ from a plain program's by a relative error of at most 0.01.
Values may be sent and summed in bfloat16 or wider, within the bound.
A program may use at most 128 MiB of HBM per device.

v0:
```python
import jax
import jax.numpy as jnp
from jax import lax
from jax.sharding import PartitionSpec as P

KERNEL_TAPS = 3
DILATION_STEP = 3


def from_behind(value, axis, by):
    devices = lax.axis_size(axis)
    return lax.ppermute(value, axis, [(i, (i + by) % devices) for i in range(devices)])


def snake_rows(rows, snake_alpha, time_mask):
    values = rows.astype(jnp.float32)
    shaped = values + jnp.sin(snake_alpha * values) ** 2 / snake_alpha
    return (shaped * time_mask[:, :, None]).astype(jnp.bfloat16)


def on_device(features, cotangent, snake_alpha, conv_weight, lengths, kept_rows, sent_rows):
    slots_in = features.shape[0]
    keep_count = slots_in // 2
    capacity = keep_count + 1
    step_total = features.shape[1]
    chan_width = features.shape[2]
    own_keep = kept_rows[0]
    own_sent = sent_rows[0]
    move_slots = jnp.arange(keep_count)
    keep_slots = jnp.arange(keep_count)
    moved_feat = lax.dynamic_slice_in_dim(features, own_keep, keep_count, 0)
    moved_cot = lax.dynamic_slice_in_dim(cotangent, own_keep, keep_count, 0)
    moved_len = jnp.where(
        move_slots < own_sent, lax.dynamic_slice_in_dim(lengths, own_keep, keep_count, 0), 0
    ).astype(jnp.bfloat16)
    arrived_feat, arrived_cot, arrived_len = from_behind(
        (moved_feat, moved_cot, moved_len), "dp", 1
    )

    def place_rows(own_part, arrived):
        blank_rows = jnp.zeros((keep_count,) + own_part.shape[1:], own_part.dtype)
        buffer = jnp.concatenate([own_part, blank_rows], axis=0)
        buffer = lax.dynamic_update_slice_in_dim(buffer, arrived, own_keep, 0)
        return buffer[:capacity]

    own_len = jnp.where(keep_slots < own_keep, lengths[:keep_count], 0)
    rows_bal = place_rows(features[:keep_count], arrived_feat)
    cot_bal = place_rows(cotangent[:keep_count], arrived_cot)
    len_bal = place_rows(own_len, arrived_len.astype(jnp.int32))
    time_mask = (jnp.arange(step_total)[None, :] < len_bal[:, None]).astype(jnp.float32)
    local_act = snake_rows(rows_bal, snake_alpha, time_mask)
    complete_output = lax.all_gather(local_act, "chan", axis=2, tiled=True)
    padded_width = complete_output.shape[2]
    padded_input = jnp.pad(complete_output, ((0, 0), (DILATION_STEP, DILATION_STEP), (0, 0)))
    flattened_rows = capacity * step_total
    shifted_tap_rows = [
        padded_input[
            :, tap_number * DILATION_STEP : tap_number * DILATION_STEP + step_total, :
        ].reshape(flattened_rows, padded_width)
        for tap_number in range(KERNEL_TAPS)
    ]
    running = jnp.zeros((flattened_rows, chan_width), jnp.float32)
    panel_rows = lax.all_gather(conv_weight, "dp", axis=0, tiled=True)
    for tap_number in range(KERNEL_TAPS):
        columns = shifted_tap_rows[tap_number]
        running = running + jnp.dot(
            columns, panel_rows[:, tap_number, :], preferred_element_type=jnp.float32
        )
    result = (
        rows_bal.astype(jnp.float32) + running.reshape(capacity, step_total, chan_width)
    ) * time_mask[:, :, None]
    balanced_out = result.astype(jnp.bfloat16)
    cot_mask = jnp.where(time_mask[:, :, None] > 0.0, cot_bal, jnp.zeros_like(cot_bal)).reshape(
        flattened_rows, chan_width
    )
    products = []
    for tap_number in range(KERNEL_TAPS):
        columns = shifted_tap_rows[tap_number]
        products.append(
            lax.dot_general(
                columns, cot_mask, (((0,), (0,)), ((), ())), preferred_element_type=jnp.float32
            )
        )
    shard_sum = lax.psum_scatter(
        jnp.stack(products, axis=1).astype(jnp.bfloat16), "dp", scatter_dimension=0, tiled=True
    )
    weight_grad = lax.psum(shard_sum, "sub").astype(jnp.float32)
    return (balanced_out, weight_grad)


def solution(mesh):
    placed = (
        P(("groups", "dp", "sub"), None, "chan"),
        P(("groups", "dp", "sub"), None, "chan"),
        P("chan"),
        P("dp", None, "chan"),
        P(("groups", "dp", "sub")),
        P(("groups", "dp", "sub")),
        P(("groups", "dp", "sub")),
    )
    return jax.shard_map(
        on_device,
        mesh=mesh,
        in_specs=placed,
        out_specs=(P(("groups", "dp", "sub"), None, "chan"), P(("groups", "dp"), None, "chan")),
        check_vma=False,
    )
```

profile of v0, /device:TPU:11, one launch (start us, length us, event | category | flops | bytes accessed | tf_op | source)
XLA Modules:
  0.0 382.6 jit_solution(10857712576062909988)
XLA Ops:
  7.2 0.0 all-gather.3.cloned.1.call-start
  7.9 3.0 copy.18
  10.9 0.0 copy-start
  10.9 1.2 constant_dynamic-slice_fusion.1
  12.1 1.3 collective-permute-start
  14.1 0.1 fusion.17
  14.2 1.3 collective-permute-start.1
  15.5 3.0 copy.24
  18.5 0.0 copy-start.7
  18.5 3.5 broadcast_select_fusion
  22.0 17.2 %collective-permute-done.1 = bf16[6]{0:T(256)(128)(2,1)S(1)} collective-permute-done((bf16[6]{0:T(256)(128)(2,1)S(1)}, bf16[6]{0:T(256)(128)(2,1)S(1)}, u32[]{:S(2)}, u32[]{:S(2)}) %collective-permute-start.1) | collective-permute-done | bytes 44 | tf_op jit(solution)/shard_map/ppermute | solution.py:12
  39.2 0.1 convert_dynamic-update-slice_fusion
  39.3 0.1 broadcast_compare_fusion
  39.3 0.0 collective-permute-done
  39.4 0.2 constant_dynamic-update-slice_fusion.1
  39.5 1.4 copy-done.1
  40.9 10.8 %fusion.7 = bf16[7,128,768]{1,2,0:T(8,128)(2,1)} fusion(f32[7,128]{1,0:T(8,128)S(1)} %get-tuple-element.9, f32[768]{0:T(1024)S(1)} %copy-done.7, bf16[12,128,768]{1,2,0:T(8,128)(2,1)S(1)} %constant_dynamic-update-slice_fusion.1), kind=kLoop, calls=%fused_computation.16 | loop fusion | flops 4816896 | bytes 2759168 | tf_op jit(solution)/shard_map/convert_element_type | solution.py:18
  51.7 0.0 all-gather.3.cloned.1.call-update
  51.7 0.0 all-gather.5.cloned.1.call-start
  51.8 0.7 all-gather.5.cloned.1.call-update
  52.5 0.0 reduce-scatter.2.cloned.1.call-start
  52.5 0.1 constant_dynamic-slice_fusion
  52.6 1.3 collective-permute-start.2
  54.0 25.6 %collective-permute-done.2 = bf16[6,128,768]{1,2,0:T(8,128)(2,1)S(1)} collective-permute-done((bf16[6,128,768]{1,2,0:T(8,128)(2,1)S(1)}, bf16[6,128,768]{1,2,0:T(8,128)(2,1)S(1)}, u32[]{:S(2)}, u32[]{:S(2)}) %collective-permute-start.2) | collective-permute-done | bytes 1179680 | tf_op jit(solution)/shard_map/ppermute | solution.py:12
  79.6 1.1 constant_dynamic-update-slice_fusion
  80.7 12.8 %all-gather.3.cloned.1.call-done = bf16[7,128,1536]{1,2,0:T(8,128)(2,1)} async-done(((bf16[7,128,768]{1,2,0:T(8,128)(2,1)}), bf16[7,128,1536]{1,2,0:T(8,128)(2,1)}) %all-gather.3.cloned.1.call-update) | async-done | bytes 2752528 | tf_op jit(solution)/shard_map/all_gather | solution.py:52
  93.5 5.0 %fusion = bf16[1536,1,768]{2,0,1:T(8,128)(2,1)S(1)} fusion(bf16[12,128,768]{1,2,0:T(8,128)(2,1)} %constant_dynamic-update-slice_fusion, pred[7,128]{1,0:T(8,128)(4,1)S(1)} %get-tuple-element.8, bf16[7,128,1536]{1,2,0:T(8,128)(2,1)} %all-gather.3.cloned.1.call-done), kind=kOutput, calls=%fused_computation.9 | convolution fusion | flops 2115796992 | bytes 6488960 | tf_op jit(solution)/shard_map/dot_general | solution.py:80
  98.5 2.9 fusion.2
  101.5 2.9 fusion.1
  104.3 3.5 pad_maximum_fusion
  107.8 0.0 reduce-scatter.2.cloned.1.call-update
  107.8 0.2 all-reduce.4.cloned.1.call-start
  108.1 3.3 pad_slice_fusion.1
  111.3 4.6 %copy.22 = bf16[7,128,1536]{2,1,0:T(8,128)(2,1)} copy(bf16[7,128,1536]{1,2,0:T(8,128)(2,1)} %get-tuple-element.7) | data formatting | bytes 5505024 | tf_op jit(solution)/shard_map/slice | solution.py:57
  115.9 4.7 %copy.20 = bf16[7,128,1536]{2,1,0:T(8,128)(2,1)} copy(bf16[7,128,1536]{1,2,0:T(8,128)(2,1)} %get-tuple-element.6) | data formatting | bytes 5505024 | tf_op jit(solution)/shard_map/slice | solution.py:57
  120.6 2.8 copy.21
  123.5 98.0 %all-gather.5.cloned.1.call-done = bf16[1536,3,768]{2,0,1:T(8,128)(2,1)} async-done(((bf16[384,3,768]{2,0,1:T(8,128)(2,1)}), bf16[1536,3,768]{2,0,1:T(8,128)(2,1)}) %all-gather.5.cloned.1.call-update) | async-done | bytes 7077904 | tf_op jit(solution)/shard_map/all_gather | solution.py:63
  221.5 6.5 %fusion.10 = f32[896,768]{1,0:T(8,128)} fusion(bf16[896,1536]{1,0:T(8,128)(2,1)} %bitcast.47, bf16[1536,3,768]{2,0,1:T(8,128)(2,1)} %all-gather.5.cloned.1.call-done), kind=kOutput, calls=%fused_computation.21 | convolution fusion | flops 2113929216 | bytes 7864320 | tf_op jit(solution)/shard_map/dot_general | solution.py:66
  228.0 120.4 %reduce-scatter.2.cloned.1.call-done = bf16[384,3,768]{2,0,1:T(8,128)(2,1)} async-done(((bf16[1536,3,768]{2,0,1:T(8,128)(2,1)}), bf16[384,3,768]{2,0,1:T(8,128)(2,1)}) %reduce-scatter.2.cloned.1.call-update) | async-done | bytes 1769488 | tf_op jit(solution)/shard_map/reduce_scatter | solution.py:84
  348.3 0.0 all-reduce.4.cloned.1.call-update
  348.4 0.0 copy-start.10
  348.4 4.1 %fusion.11 = f32[896,768]{1,0:T(8,128)S(1)} fusion(bf16[896,1536]{1,0:T(8,128)(2,1)S(1)} %bitcast.46, bf16[1536,3,768]{2,0,1:T(8,128)(2,1)} %all-gather.5.cloned.1.call-done), kind=kOutput, calls=%fused_computation.23 | convolution fusion | flops 2113929216 | bytes 7864320 | tf_op jit(solution)/shard_map/dot_general | solution.py:66
  352.5 5.5 %add_add_fusion = f32[896,768]{1,0:T(8,128)} fusion(f32[896,768]{1,0:T(8,128)S(1)} %copy-done.10, f32[896,768]{1,0:T(8,128)S(1)} %fusion.11, bf16[896,1536]{1,0:T(8,128)(2,1)S(1)} %bitcast.45, bf16[1536,3,768]{2,0,1:T(8,128)(2,1)} %all-gather.5.cloned.1.call-done), kind=kOutput, calls=%fused_computation.19 | convolution fusion | flops 2115305472 | bytes 13369344 | tf_op jit(solution)/shard_map/dot_general | solution.py:66
  358.0 3.5 copy.23
  361.5 3.2 fusion.9
  364.7 2.5 copy.29
  367.2 5.2 %all-reduce.4.cloned.1.call-done = bf16[384,3,768]{2,0,1:T(8,128)(2,1)} async-done(((bf16[384,3,768]{2,0,1:T(8,128)(2,1)}), bf16[384,3,768]{2,0,1:T(8,128)(2,1)}) %all-reduce.4.cloned.1.call-update) | async-done | bytes 1769488 | tf_op jit(solution)/shard_map/psum | solution.py:87
  372.5 3.6 convert_element_type.38
  (19 shorter events, 0.0 us)
Async XLA Ops:
  7.2 86.4 %all-gather.3.cloned.1.call-start = ((), (), s32[]{:S(2)}) async-start(), calls=%async_computation.1 | async-start | bytes 4128768 | tf_op jit(solution)/shard_map/all_gather | solution.py:52
  7.9 6.2 %copy-start.8 = (s32[12]{0:T(128)S(1)}, s32[12]{0:T(128)}, u32[]{:S(2)}) copy-start(s32[12]{0:T(128)} %param.11) | copy-start | bytes 148
  10.9 4.6 %copy-start = (bf16[12,128,768]{1,2,0:T(8,128)(2,1)}, bf16[12,128,768]{1,2,0:T(8,128)(2,1)S(1)}, u32[]{:S(2)}) copy-start(bf16[12,128,768]{1,2,0:T(8,128)(2,1)S(1)} %copy.18) | copy-start | bytes 7077892
  12.1 6.4 %copy-start.9 = (pred[12]{0:T(512)(128)(4,1)S(1)}, pred[12]{0:T(512)(128)(4,1)}, u32[]{:S(2)}) copy-start(pred[12]{0:T(512)(128)(4,1)} %constant.5.clone.1) | copy-start | bytes 40
  12.1 27.2 %collective-permute-start = (bf16[6,128,768]{1,2,0:T(8,128)(2,1)}, bf16[6,128,768]{1,2,0:T(8,128)(2,1)S(1)}, u32[]{:S(2)}, u32[]{:S(2)}) collective-permute-start(bf16[6,128,768]{1,2,0:T(8,128)(2,1)} %constant_dynamic-slice_fusion.1), channel_id=1, source_target_pairs={{0,4},{4,8},{8,12},{12,0},{1,5},{5,9},{9,13},{13,1},{2,6},{6,10},{... | collective-permute-start | bytes 3538952 | tf_op jit(solution)/shard_map/ppermute | solution.py:12
  14.2 25.0 %collective-permute-start.1 = (bf16[6]{0:T(256)(128)(2,1)S(1)}, bf16[6]{0:T(256)(128)(2,1)S(1)}, u32[]{:S(2)}, u32[]{:S(2)}) collective-permute-start(bf16[6]{0:T(256)(128)(2,1)S(1)} %get-tuple-element.12), channel_id=1, source_target_pairs={{0,4},{4,8},{8,12},{12,0},{1,5},{5,9},{9,13},{13,1},{2,6},{6,10},{... | collective-permute-start | bytes 44 | tf_op jit(solution)/shard_map/ppermute | solution.py:12
  18.5 22.4 %copy-start.7 = (f32[768]{0:T(1024)S(1)}, f32[768]{0:T(1024)}, u32[]{:S(2)}) copy-start(f32[768]{0:T(1024)} %param.9) | copy-start | bytes 9220
  39.5 1.4 copy-start.1
  51.7 169.8 %all-gather.5.cloned.1.call-start = ((), (), s32[]{:S(2)}) async-start(), calls=%async_computation.2 | async-start | bytes 8847360 | tf_op jit(solution)/shard_map/all_gather | solution.py:63
  52.5 295.9 %reduce-scatter.2.cloned.1.call-start = ((), (), s32[]{:S(2)}) async-start(), calls=%async_computation.3 | async-start | bytes 8847360 | tf_op jit(solution)/shard_map/reduce_scatter | solution.py:84
  52.6 27.0 %collective-permute-start.2 = (bf16[6,128,768]{1,2,0:T(8,128)(2,1)S(1)}, bf16[6,128,768]{1,2,0:T(8,128)(2,1)S(1)}, u32[]{:S(2)}, u32[]{:S(2)}) collective-permute-start(bf16[6,128,768]{1,2,0:T(8,128)(2,1)S(1)} %constant_dynamic-slice_fusion), channel_id=1, source_target_pairs={{0,4},{4,8},{8,12},{12,0},{1,5},{5,9},{9,13},{13,1},{2,6},{6,10},{... | collective-permute-start | bytes 3538952 | tf_op jit(solution)/shard_map/ppermute | solution.py:12
  93.5 5.0 %copy-start.3 = (bf16[7,128,1536]{1,2,0:T(8,128)(2,1)S(1)}, bf16[7,128,1536]{1,2,0:T(8,128)(2,1)}, u32[]{:S(2)}) copy-start(bf16[7,128,1536]{1,2,0:T(8,128)(2,1)} %all-gather.3.cloned.1.call-done) | copy-start | bytes 8257540
  93.5 5.0 %copy-start.6 = (bf16[12,128,768]{1,2,0:T(8,128)(2,1)S(1)}, bf16[12,128,768]{1,2,0:T(8,128)(2,1)}, u32[]{:S(2)}) copy-start(bf16[12,128,768]{1,2,0:T(8,128)(2,1)} %constant_dynamic-update-slice_fusion) | copy-start | bytes 7077892
  107.8 264.7 %all-reduce.4.cloned.1.call-start = ((), (), s32[]{:S(2)}) async-start(), calls=%async_computation.4 | async-start | bytes 3538944 | tf_op jit(solution)/shard_map/psum | solution.py:87
  221.5 126.9 %copy-start.5 = (bf16[7,128,1536]{2,1,0:T(8,128)(2,1)S(1)}, bf16[7,128,1536]{2,1,0:T(8,128)(2,1)}, u32[]{:S(2)}) copy-start(bf16[7,128,1536]{2,1,0:T(8,128)(2,1)} %copy.21) | copy-start | bytes 8257540
  348.4 4.1 %copy-start.4 = (bf16[7,128,1536]{2,1,0:T(8,128)(2,1)S(1)}, bf16[7,128,1536]{2,1,0:T(8,128)(2,1)}, u32[]{:S(2)}) copy-start(bf16[7,128,1536]{2,1,0:T(8,128)(2,1)} %copy.20) | copy-start | bytes 8257540
  348.4 4.1 %copy-start.10 = (f32[896,768]{1,0:T(8,128)S(1)}, f32[896,768]{1,0:T(8,128)}, u32[]{:S(2)}) copy-start(f32[896,768]{1,0:T(8,128)} %fusion.10) | copy-start | bytes 8257540
  358.0 3.5 copy-start.2
Sparse Core Ops, SparseCore 0:
  51.8 41.6 all-gather.2
  95.1 126.3 all-gather.4
  223.8 124.4 reduce-scatter.1
  350.6 21.8 all-reduce.3
where the time goes:
time: 384 us; the launch traced here: 383 us
  waiting for transfers between devices  280 us (73%)
  local copies, waits for them, and re-layouts  31.5 us (8%)
  matrix products  26.9 us (7%)
  other arithmetic  24.7 us (6%)
  between operations  15.2 us (4%)
  starting transfers between devices  4.28 us (1%)
    reduce_scatter x1, waiting for transfers between devices, on_device(): lax.psum_scatter(jnp.stack(products, axis=1).astype(jnp.bfloat16), 'dp',...  120 us
    all_gather x1, waiting for transfers between devices, on_device(): panel_rows = lax.all_gather(conv_weight, 'dp', axis=0, tiled=True)  98 us
    ppermute x3, waiting for transfers between devices, from_behind(): lax.ppermute(value, axis, [(i, (i + by) % devices) for i in range(devices)])  42.8 us
    dot_general x3, matrix products, on_device(): jnp.dot(columns, panel_rows[:, tap_number, :], preferred_element_type=jnp...  16.1 us
    all_gather x1, waiting for transfers between devices, on_device(): complete_output = lax.all_gather(local_act, 'chan', axis=2, tiled=True)  12.8 us
    slice x3, local copies, waits for them, and re-layouts, on_device(): padded_input[:, tap_number * DILATION_STEP:tap_number * DILATION_STEP + s...  12.6 us
    dot_general x3, matrix products, on_device(): lax.dot_general(columns, cot_mask, (((0,), (0,)), ((), ())), preferred_el...  10.8 us
    convert_element_type x1, other arithmetic, snake_rows(): return (shaped * time_mask[:, :, None]).astype(jnp.bfloat16)  10.8 us
  transfers between devices with their start and end apart: 7, of which 6 were waited for; matrix products, arithmetic and copies ran while one was open for 16% of the time, Pallas kernels for 0%

commit v1 on v0

--- a/solution.py
+++ b/solution.py
@@ -1,6 +1,10 @@
+import functools
+
 import jax
 import jax.numpy as jnp
 from jax import lax
+from jax.experimental import pallas as pl
+from jax.experimental.pallas import tpu as pltpu
 from jax.sharding import PartitionSpec as P
 
 KERNEL_TAPS = 3
@@ -88,6 +92,365 @@
     return (balanced_out, weight_grad)
 
 
+PI_HIGH = 3.140625
+PI_LOW = 9.67653589793e-4
+SINE = (-1.0 / 6, 1.0 / 120, -1.0 / 5040, 1.0 / 362880, -1.0 / 39916800)
+MESH = pl.DeviceIdType.MESH
+
+
+def sine_squared(z):
+    turns = jnp.floor(z * (1.0 / 3.14159265358979) + 0.5)
+    r = (z - turns * PI_HIGH) - turns * PI_LOW
+    r2 = r * r
+    poly = SINE[4]
+    for coefficient in (SINE[3], SINE[2], SINE[1], SINE[0]):
+        poly = poly * r2 + coefficient
+    s = r + r * (r2 * poly)
+    return s * s
+
+
+def fused_kernel(
+    n, feat, cot, alpha, weight, lengths, kept, sent,
+    bal, gout,
+    act_all, cot3, wg, own, stage, sib_in, rs_in, rs_right, y_buf, out_full, rows_out, rows_in,
+    x_send, x_recv, w_send, w_recv, ws_send, ws_recv, w_local,
+    g_send, g_recv, r_send, r_recv, rr_recv, f_send, f_recv, o_send, o_recv,
+):
+    d = lax.axis_index("dp")
+    c = lax.axis_index("chan")
+    s = lax.axis_index("sub")
+    slots, steps, width = feat.shape
+    depth = weight.shape[1]
+    half_depth = depth // 2
+    half = width // 2
+    sib = {"sub": 1 - s}
+
+    def remote(src, dst, send_sem, recv_sem, to):
+        return pltpu.make_async_remote_copy(
+            src_ref=src, dst_ref=dst, send_sem=send_sem, recv_sem=recv_sem,
+            device_id=to, device_id_type=MESH,
+        )
+
+    right_ring = lax.rem(d + 1, n)
+    left_ring = lax.rem(d + n - 1, n)
+    barrier = pltpu.get_barrier_semaphore()
+    for peer in (sib, {"chan": 1 - c}, {"dp": right_ring}, {"dp": left_ring}):
+        pl.semaphore_signal(barrier, inc=1, device_id=peer, device_id_type=MESH)
+    pl.semaphore_wait(barrier, 4)
+
+    def w_part(src):
+        return wg.at[:, pl.ds(pl.multiple_of(src * depth + s * half_depth, 16), half_depth), :]
+
+    def w_source(way, k):
+        return d - k if way == 0 else d + k
+
+    def w_hop(way, k):
+        src = w_source(way, k)
+        if k == 0:
+            ref = weight.at[:, pl.ds(pl.multiple_of(s * half_depth, 16), half_depth), :]
+        else:
+            ref = w_part(src)
+        to = d + 1 if way == 0 else d - 1
+        return remote(ref, w_part(src), w_send.at[way, k], w_recv.at[way, k], {"dp": to})
+
+    def w_share(way, k):
+        part = w_part(w_source(way, k))
+        return remote(part, part, ws_send.at[way, k], ws_recv.at[way, k], sib)
+
+    def w_exists(way, k):
+        return d - k >= 0 if way == 0 else d + k <= n - 1
+
+    def w_more(way):
+        return d < n - 1 if way == 0 else d > 0
+
+    def w_start():
+        for way in range(2):
+            @pl.when(w_more(way))
+            def _(way=way):
+                w_hop(way, 0).start()
+
+    def w_forward(k):
+        for way in range(2):
+            @pl.when(w_exists(way, k))
+            def _(way=way):
+                w_hop(way, k - 1).wait_recv()
+                w_share(way, k).start()
+
+            if k < n - 1:
+                @pl.when(jnp.logical_and(w_exists(way, k), w_more(way)))
+                def _(way=way):
+                    w_hop(way, k).start()
+
+    own_weight = pltpu.make_async_copy(
+        weight, wg.at[:, pl.ds(pl.multiple_of(d * depth, 16), depth), :], w_local
+    )
+
+    def w_finish():
+        own_weight.wait()
+        for k in range(1, n):
+            for way in range(2):
+                @pl.when(w_exists(way, k))
+                def _(way=way, k=k):
+                    w_share(way, k).wait_recv()
+
+    w_start()
+    own_weight.start()
+
+    filled = kept[0] + sent[0]
+
+    def slot_length(r):
+        return jnp.where(r < filled, lengths[r], 0)
+
+    def x_copy(r):
+        part = act_all.at[
+            pl.ds(pl.multiple_of(r * steps, steps), steps),
+            pl.ds(pl.multiple_of(c * width, width), width),
+        ]
+        return remote(part, part, x_send.at[r], x_recv.at[r], {"chan": 1 - c})
+
+    tile = 128
+    time = lax.broadcasted_iota(jnp.int32, (steps, tile), 0)
+
+    def act_row(r, carry):
+        mask = time < slot_length(r)
+        at = pl.ds(pl.multiple_of(r * steps, steps), steps)
+        for j in range(width // tile):
+            cols = pl.ds(j * tile, tile)
+            x = feat[r, :, cols].astype(jnp.float32)
+            a = alpha[:, cols]
+            shaped = x + sine_squared(a * x) * (1.0 / a)
+            act_all[at, pl.ds(pl.multiple_of(c * width + j * tile, tile), tile)] = jnp.where(
+                mask, shaped, 0.0
+            ).astype(jnp.bfloat16)
+        x_copy(r).start()
+        for j in range(width // tile):
+            cols = pl.ds(j * tile, tile)
+            v = jnp.where(mask, cot[r, :, cols].astype(jnp.float32), 0.0)
+            h, at_col = (j * tile) // half, (j * tile) % half
+            early = jnp.where(
+                time < steps - DILATION_STEP, pltpu.roll(v, steps - DILATION_STEP, 0), 0.0
+            )
+            late = jnp.where(time >= DILATION_STEP, pltpu.roll(v, DILATION_STEP, 0), 0.0)
+            for q, value in enumerate((early, v, late)):
+                cot3[h, at, pl.ds(q * half + at_col, tile)] = value.astype(jnp.bfloat16)
+        return carry
+
+    lax.fori_loop(0, slots, act_row, 0)
+
+    def chunk(k):
+        first = (0, 1, 3, 2)[k]
+        return first + c * (3 - 2 * first)
+
+    def g_copy(e):
+        return remote(stage.at[e], sib_in.at[e], g_send.at[e], g_recv.at[e], sib)
+
+    def grad(k):
+        e = chunk(k)
+        lhs = pl.ds(pl.multiple_of(e * depth, 128), depth)
+        dims = (((0,), (0,)), ((), ()))
+        stage[e] = lax.dot_general(
+            act_all[:, lhs], cot3[1 - s], dims, preferred_element_type=jnp.float32
+        ).astype(jnp.bfloat16)
+        g_copy(e).start()
+        own[e] = lax.dot_general(
+            act_all[:, lhs], cot3[s], dims, preferred_element_type=jnp.float32
+        )
+
+    def r_copy(e, q, way):
+        cols = pl.ds(q * half, half)
+        src = sib_in.at[e, :, cols]
+        if way == 0:
+            return remote(src, rs_in.at[e, :, cols], r_send.at[e, q], r_recv.at[e, q], {"dp": d + 1})
+        if way == 1:
+            return remote(src, rs_in.at[e, :, cols], r_send.at[e, q], r_recv.at[e, q], {"dp": d - 1})
+        return remote(src, rs_right.at[:, cols], r_send.at[e, q], rr_recv.at[q], {"dp": d - 1})
+
+    def f_copy(q):
+        cols = pl.ds(pl.multiple_of(s * half, half), half)
+        part = gout.at[q, :, cols]
+        return remote(part, part, f_send.at[q], f_recv.at[q], sib)
+
+    def reduce_step(k, q):
+        e = chunk(k)
+        cols = pl.ds(q * half, half)
+        if q == 0:
+            g_copy(e).wait_recv()
+        enters = jnp.logical_or(
+            jnp.logical_and(d <= e, d > 0), jnp.logical_and(d > e, d < n - 1)
+        )
+
+        @pl.when(enters)
+        def _():
+            r_copy(e, q, 0).wait_recv()
+            own[e, :, cols] = own[e, :, cols] + rs_in[e, :, cols].astype(jnp.float32)
+
+        @pl.when(jnp.logical_and(d == e, d < n - 1))
+        def _():
+            r_copy(e, q, 2).wait_recv()
+            own[e, :, cols] = own[e, :, cols] + rs_right[:, cols].astype(jnp.float32)
+
+        total = own[e, :, cols] + sib_in[e, :, cols].astype(jnp.float32)
+
+        @pl.when(d != e)
+        def _():
+            sib_in[e, :, cols] = total.astype(jnp.bfloat16)
+
+        @pl.when(d < e)
+        def _():
+            r_copy(e, q, 0).start()
+
+        @pl.when(d > e + 1)
+        def _():
+            r_copy(e, q, 1).start()
+
+        @pl.when(d == e + 1)
+        def _():
+            r_copy(e, q, 2).start()
+
+        @pl.when(d == e)
+        def _():
+            gout[q, :, pl.ds(pl.multiple_of(s * half, half), half)] = total
+            f_copy(q).start()
+
+    group = y_buf.shape[1] // steps
+
+    def conv(g):
+        at = pl.ds(g * group * steps, group * steps)
+        for q in range(KERNEL_TAPS):
+            y_buf[q] = jnp.dot(act_all[at, :], wg[q], preferred_element_type=jnp.float32)
+
+        def finish(i, carry):
+            r = g * group + i
+            mask = time < slot_length(r)
+            rows = pl.ds(pl.multiple_of(i * steps, steps), steps)
+            for j in range(width // tile):
+                cols = pl.ds(j * tile, tile)
+                before = jnp.where(
+                    time >= DILATION_STEP, pltpu.roll(y_buf[0, rows, cols], DILATION_STEP, 0), 0.0
+                )
+                after = jnp.where(
+                    time < steps - DILATION_STEP,
+                    pltpu.roll(y_buf[2, rows, cols], steps - DILATION_STEP, 0),
+                    0.0,
+                )
+                value = feat[r, :, cols].astype(jnp.float32) + (before + y_buf[1, rows, cols] + after)
+                out_full[r, :, cols] = jnp.where(mask, value, 0.0).astype(jnp.bfloat16)
+            return carry
+
+        lax.fori_loop(0, group, finish, 0)
+
+    grad(0)
+    grad(1)
+    w_forward(1)
+    for q in range(KERNEL_TAPS):
+        reduce_step(0, q)
+    for r in range(slots):
+        x_copy(r).wait_recv()
+    w_forward(2)
+    grad(2)
+    grad(3)
+    for q in range(KERNEL_TAPS):
+        reduce_step(1, q)
+    w_forward(3)
+    w_finish()
+    groups = slots // group
+    conv(0)
+    for q in range(KERNEL_TAPS):
+        reduce_step(2, q)
+    for g in range(1, groups):
+        conv(g)
+    own_keep = kept[0]
+    moved = rows_out.shape[0]
+    for j in range(moved):
+        rows_out[j] = out_full[own_keep + j]
+    o_copy = remote(rows_out, rows_in, o_send, o_recv, {"dp": right_ring})
+    o_copy.start()
+    for q in range(KERNEL_TAPS):
+        reduce_step(3, q)
+    o_copy.wait_recv()
+    for j in range(bal.shape[0]):
+        arrived = rows_in[jnp.clip(j - own_keep, 0, moved - 1)]
+        if j < moved:
+            bal[j] = jnp.where(j < own_keep, out_full[j], arrived)
+        else:
+            bal[j] = arrived
+    for q in range(KERNEL_TAPS):
+        f_copy(q).wait_recv()
+
+    for r in range(slots):
+        x_copy(r).wait_send()
+    for way in range(2):
+        for k in range(n):
+            if k < n - 1:
+                @pl.when(jnp.logical_and(w_exists(way, k), w_more(way)))
+                def _(way=way, k=k):
+                    w_hop(way, k).wait_send()
+            if k > 0:
+                @pl.when(w_exists(way, k))
+                def _(way=way, k=k):
+                    w_share(way, k).wait_send()
+    for k in range(n):
+        e = chunk(k)
+        g_copy(e).wait_send()
+
+        @pl.when(d != e)
+        def _(e=e):
+            for q in range(KERNEL_TAPS):
+                r_copy(e, q, 0).wait_send()
+    for q in range(KERNEL_TAPS):
+        f_copy(q).wait_send()
+    o_copy.wait_send()
+
+
+def fused_on_device(features, cotangent, snake_alpha, conv_weight, lengths, kept_rows, sent_rows):
+    n = lax.axis_size("dp")
+    slots, steps, width = features.shape
+    depth = conv_weight.shape[0]
+    total = 2 * width
+    moved = slots // 2
+    group = 4
+    bf16, f32 = jnp.bfloat16, jnp.float32
+    vmem = pl.BlockSpec(memory_space=pltpu.VMEM)
+    smem = pl.BlockSpec(memory_space=pltpu.SMEM)
+    dma = pltpu.SemaphoreType.DMA
+    wide = KERNEL_TAPS * width // 2
+    weight = jnp.transpose(conv_weight, (1, 0, 2))
+    flops = 2 * 2 * slots * steps * total * KERNEL_TAPS * width
+    bal, gout = pl.pallas_call(
+        functools.partial(fused_kernel, n),
+        out_shape=(
+            jax.ShapeDtypeStruct((moved + 1, steps, width), bf16),
+            jax.ShapeDtypeStruct((KERNEL_TAPS, depth, width), f32),
+        ),
+        in_specs=[vmem] * 4 + [smem] * 3,
+        out_specs=(vmem, vmem),
+        scratch_shapes=[
+            pltpu.VMEM((slots * steps, total), bf16),
+            pltpu.VMEM((2, slots * steps, wide), bf16),
+            pltpu.VMEM((KERNEL_TAPS, total, width), bf16),
+            pltpu.VMEM((n, depth, wide), f32),
+            pltpu.VMEM((n, depth, wide), bf16),
+            pltpu.VMEM((n, depth, wide), bf16),
+            pltpu.VMEM((n, depth, wide), bf16),
+            pltpu.VMEM((depth, wide), bf16),
+            pltpu.VMEM((KERNEL_TAPS, group * steps, width), f32),
+            pltpu.VMEM((slots, steps, width), bf16),
+            pltpu.VMEM((moved, steps, width), bf16),
+            pltpu.VMEM((moved, steps, width), bf16),
+            dma((slots,)), dma((slots,)),
+            dma((2, n)), dma((2, n)), dma((2, n)), dma((2, n)), dma,
+            dma((n,)), dma((n,)), dma((n, KERNEL_TAPS)), dma((n, KERNEL_TAPS)), dma((KERNEL_TAPS,)),
+            dma((KERNEL_TAPS,)), dma((KERNEL_TAPS,)), dma, dma,
+        ],
+        compiler_params=pltpu.CompilerParams(
+            collective_id=0, has_side_effects=True, vmem_limit_bytes=63 * 1024 * 1024
+        ),
+        cost_estimate=pl.CostEstimate(flops=flops, bytes_accessed=16 * 2**20, transcendentals=0),
+        name="snake_conv_fused",
+    )(features, cotangent, snake_alpha[None, :], weight, lengths, kept_rows, sent_rows)
+    return bal, jnp.transpose(gout, (1, 0, 2))
+
+
 def solution(mesh):
     placed = (
         P(("groups", "dp", "sub"), None, "chan"),
@@ -98,8 +461,9 @@
         P(("groups", "dp", "sub")),
         P(("groups", "dp", "sub")),
     )
+    fits = mesh.shape["dp"] == 4 and mesh.shape["chan"] == 2
     return jax.shard_map(
-        on_device,
+        fused_on_device if fits else on_device,
         mesh=mesh,
         in_specs=placed,
         out_specs=(P(("groups", "dp", "sub"), None, "chan"), P(("groups", "dp"), None, "chan")),

time: 384 us -> 232 us (0.60)
  waiting for transfers between devices: 280 us -> 0 us
  Pallas kernels: 0 us -> 222 us
  matrix products: 26.9 us -> 0 us
  other arithmetic: 24.7 us -> 0 us
  local copies, waits for them, and re-layouts: 31.5 us -> 7.79 us
  between operations: 15.2 us -> 1.93 us
  starting transfers between devices: 4.28 us -> 0 us
    pallas_call x0 -> x1, Pallas kernels: none -> 222 us  [fused_on_device(): pl.pallas_call(functools.partial(fused_kernel, n), out_shape=(jax.ShapeDt...]
    reduce_scatter x1 -> x0, waiting for transfers between devices: 120 us -> none  [on_device(): lax.psum_scatter(jnp.stack(products, axis=1).astype(jnp.bfloat16), 'dp',...]
    all_gather x2 -> x0, waiting for transfers between devices: 111 us -> none  [the longest x1 98 us: on_device(): panel_rows = lax.all_gather(conv_weight, 'dp', axis=0, tiled=True)]
    ppermute x3 -> x0, waiting for transfers between devices: 42.8 us -> none  [from_behind(): lax.ppermute(value, axis, [(i, (i + by) % devices) for i in range(devices)])]
    dot_general x6 -> x0, matrix products: 26.9 us -> none  [the longest x3 16.1 us: on_device(): jnp.dot(columns, panel_rows[:, tap_number, :], preferred_element_type=jnp...]
    convert_element_type x4 -> x0, other arithmetic: 17.6 us -> none  [the longest x1 10.8 us: snake_rows(): return (shaped * time_mask[:, :, None]).astype(jnp.bfloat16)]
    slice x3 -> x0, local copies, waits for them, and re-layouts: 12.6 us -> none  [on_device(): padded_input[:, tap_number * DILATION_STEP:tap_number * DILATION_STEP + s...]
    psum x1 -> x0, waiting for transfers between devices: 5.25 us -> none  [on_device(): weight_grad = lax.psum(shard_sum, 'sub').astype(jnp.float32)]
  transfers between devices with their start and end apart: 7 -> 0, of which waited for: 6 -> 0; matrix products, arithmetic and copies ran while one was open for 16% -> 0% of each run, Pallas kernels for 0% -> 0%
where the time goes in v1:
time: 232 us; the launch traced here: 231 us
  Pallas kernels  222 us (96%)
  local copies, waits for them, and re-layouts  7.79 us (3%)
    pallas_call x1, Pallas kernels, fused_on_device(): pl.pallas_call(functools.partial(fused_kernel, n), out_shape=(jax.ShapeDt...  222 us
    unnamed x2, local copies, waits for them, and re-layouts  6.53 us

profile of v1, /device:TPU:11, one launch (start us, length us, event | category | flops | bytes accessed | tf_op | source)
XLA Modules:
  0.0 231.4 jit_solution(13722680528379470798)
XLA Ops:
  1.9 1.3 broadcast_in_dim.3.alpha
  3.2 221.7 %snake_conv_fused.1 = (bf16[7,128,768]{2,1,0:T(8,128)(2,1)}, f32[3,384,768]{2,1,0:T(8,128)}) custom-call(bf16[12,128,768]{2,1,0:T(8,128)(2,1)} %feat.1, bf16[12,128,768]{2,1,0:T(8,128)(2,1)} %cot.1, f32[1,768]{1,0:T(1,128)} %broadcast_in_dim.3.alpha, bf16[3,384,768]{2,1,0:T(8,128)(2,1)} %bitcast.3, s32[12]{0:T(128)} %lengths.1, s32[1]{0:T(128)S(6)} %copy.11.kept, ...), custom_call_target="tpu_custom_call" | custom-call | flops 21743271936 | bytes 16777216 | tf_op jit(solution)/shard_map/snake_conv_fused/pallas_call | solution.py:419
  224.9 2.5 %copy.13 = bf16[7,128,768]{2,1,0:T(8,128)(2,1)} copy(bf16[7,128,768]{2,1,0:T(8,128)(2,1)} %get-tuple-element.8) | data formatting | bytes 2752512
  227.4 4.0 %copy.14 = f32[384,3,768]{2,0,1:T(8,128)} copy(f32[384,3,768]{2,0,1:T(8,128)} %bitcast.2) | data formatting | bytes 7077888

commit v2 on v1

--- a/solution.py
+++ b/solution.py
@@ -113,17 +113,19 @@
     n, feat, cot, alpha, weight, lengths, kept, sent,
     bal, gout,
     act_all, cot3, wg, own, stage, sib_in, rs_in, rs_right, y_buf, out_full, rows_out, rows_in,
-    x_send, x_recv, w_send, w_recv, ws_send, ws_recv, w_local,
+    x_send, x_recv, w_send, w_recv, ws_send, ws_recv, wy_send, wy_recv, wr_send, wr_recv, w_local,
     g_send, g_recv, r_send, r_recv, rr_recv, f_send, f_recv, o_send, o_recv,
 ):
     d = lax.axis_index("dp")
     c = lax.axis_index("chan")
     s = lax.axis_index("sub")
+    y = lax.axis_index("groups")
     slots, steps, width = feat.shape
     depth = weight.shape[1]
-    half_depth = depth // 2
+    quarter = depth // 4
     half = width // 2
     sib = {"sub": 1 - s}
+    across = {"groups": 1 - y}
 
     def remote(src, dst, send_sem, recv_sem, to):
         return pltpu.make_async_remote_copy(
@@ -134,12 +136,13 @@
     right_ring = lax.rem(d + 1, n)
     left_ring = lax.rem(d + n - 1, n)
     barrier = pltpu.get_barrier_semaphore()
-    for peer in (sib, {"chan": 1 - c}, {"dp": right_ring}, {"dp": left_ring}):
+    for peer in (sib, across, {"chan": 1 - c}, {"dp": right_ring}, {"dp": left_ring}):
         pl.semaphore_signal(barrier, inc=1, device_id=peer, device_id_type=MESH)
-    pl.semaphore_wait(barrier, 4)
-
-    def w_part(src):
-        return wg.at[:, pl.ds(pl.multiple_of(src * depth + s * half_depth, 16), half_depth), :]
+    pl.semaphore_wait(barrier, 5)
+
+    def w_part(src, group):
+        at = src * depth + (2 * group + s) * quarter
+        return wg.at[:, pl.ds(pl.multiple_of(at, 16), quarter), :]
 
     def w_source(way, k):
         return d - k if way == 0 else d + k
@@ -147,15 +150,23 @@
     def w_hop(way, k):
         src = w_source(way, k)
         if k == 0:
-            ref = weight.at[:, pl.ds(pl.multiple_of(s * half_depth, 16), half_depth), :]
+            ref = weight.at[:, pl.ds(pl.multiple_of((2 * y + s) * quarter, 16), quarter), :]
         else:
-            ref = w_part(src)
+            ref = w_part(src, y)
         to = d + 1 if way == 0 else d - 1
-        return remote(ref, w_part(src), w_send.at[way, k], w_recv.at[way, k], {"dp": to})
+        return remote(ref, w_part(src, y), w_send.at[way, k], w_recv.at[way, k], {"dp": to})
 
     def w_share(way, k):
-        part = w_part(w_source(way, k))
+        part = w_part(w_source(way, k), y)
         return remote(part, part, ws_send.at[way, k], ws_recv.at[way, k], sib)
+
+    def w_cross(way, k):
+        part = w_part(w_source(way, k), y)
+        return remote(part, part, wy_send.at[way, k], wy_recv.at[way, k], across)
+
+    def w_pass(way, k):
+        part = w_part(w_source(way, k), 1 - y)
+        return remote(part, part, wr_send.at[way, k], wr_recv.at[way, k], sib)
 
     def w_exists(way, k):
         return d - k >= 0 if way == 0 else d + k <= n - 1
@@ -174,12 +185,20 @@
             @pl.when(w_exists(way, k))
             def _(way=way):
                 w_hop(way, k - 1).wait_recv()
+                w_cross(way, k).start()
                 w_share(way, k).start()
 
             if k < n - 1:
                 @pl.when(jnp.logical_and(w_exists(way, k), w_more(way)))
                 def _(way=way):
                     w_hop(way, k).start()
+
+    def w_relay(k):
+        for way in range(2):
+            @pl.when(w_exists(way, k))
+            def _(way=way):
+                w_cross(way, k).wait_recv()
+                w_pass(way, k).start()
 
     own_weight = pltpu.make_async_copy(
         weight, wg.at[:, pl.ds(pl.multiple_of(d * depth, 16), depth), :], w_local
@@ -192,6 +211,7 @@
                 @pl.when(w_exists(way, k))
                 def _(way=way, k=k):
                     w_share(way, k).wait_recv()
+                    w_pass(way, k).wait_recv()
 
     w_start()
     own_weight.start()
@@ -270,6 +290,22 @@
         part = gout.at[q, :, cols]
         return remote(part, part, f_send.at[q], f_recv.at[q], sib)
 
+    def starts_chain(e):
+        return jnp.logical_or(
+            jnp.logical_and(d < e, d == 0), jnp.logical_and(d > e, d == n - 1)
+        )
+
+    def first_steps(k):
+        @pl.when(starts_chain(chunk(k)))
+        def _():
+            for q in range(KERNEL_TAPS):
+                reduce_step(k, q)
+
+    def next_step(k, q):
+        @pl.when(jnp.logical_not(starts_chain(chunk(k))))
+        def _():
+            reduce_step(k, q)
+
     def reduce_step(k, q):
         e = chunk(k)
         cols = pl.ds(q * half, half)
@@ -341,32 +377,41 @@
 
     grad(0)
     grad(1)
+    first_steps(0)
+    first_steps(1)
     w_forward(1)
-    for q in range(KERNEL_TAPS):
-        reduce_step(0, q)
+    next_step(0, 0)
+    w_relay(1)
+    w_forward(2)
     for r in range(slots):
         x_copy(r).wait_recv()
-    w_forward(2)
     grad(2)
+    first_steps(2)
     grad(3)
-    for q in range(KERNEL_TAPS):
-        reduce_step(1, q)
+    first_steps(3)
+    next_step(0, 1)
+    w_relay(2)
     w_forward(3)
+    next_step(0, 2)
+    w_relay(3)
+    next_step(1, 0)
     w_finish()
-    groups = slots // group
     conv(0)
-    for q in range(KERNEL_TAPS):
-        reduce_step(2, q)
-    for g in range(1, groups):
-        conv(g)
+    next_step(2, 0)
+    conv(1)
+    next_step(1, 1)
+    conv(2)
     own_keep = kept[0]
     moved = rows_out.shape[0]
     for j in range(moved):
         rows_out[j] = out_full[own_keep + j]
     o_copy = remote(rows_out, rows_in, o_send, o_recv, {"dp": right_ring})
     o_copy.start()
+    next_step(2, 1)
+    next_step(1, 2)
+    next_step(2, 2)
     for q in range(KERNEL_TAPS):
-        reduce_step(3, q)
+        next_step(3, q)
     o_copy.wait_recv()
     for j in range(bal.shape[0]):
         arrived = rows_in[jnp.clip(j - own_keep, 0, moved - 1)]
@@ -389,6 +434,8 @@
                 @pl.when(w_exists(way, k))
                 def _(way=way, k=k):
                     w_share(way, k).wait_send()
+                    w_cross(way, k).wait_send()
+                    w_pass(way, k).wait_send()
     for k in range(n):
         e = chunk(k)
         g_copy(e).wait_send()
@@ -438,7 +485,7 @@
             pltpu.VMEM((moved, steps, width), bf16),
             pltpu.VMEM((moved, steps, width), bf16),
             dma((slots,)), dma((slots,)),
-            dma((2, n)), dma((2, n)), dma((2, n)), dma((2, n)), dma,
+            *[dma((2, n))] * 8, dma,
             dma((n,)), dma((n,)), dma((n, KERNEL_TAPS)), dma((n, KERNEL_TAPS)), dma((KERNEL_TAPS,)),
             dma((KERNEL_TAPS,)), dma((KERNEL_TAPS,)), dma, dma,
         ],
@@ -462,6 +509,7 @@
         P(("groups", "dp", "sub")),
     )
     fits = mesh.shape["dp"] == 4 and mesh.shape["chan"] == 2
+    fits = fits and mesh.shape["groups"] == 2
     return jax.shard_map(
         fused_on_device if fits else on_device,
         mesh=mesh,

time: 232 us -> 189 us (0.81)
  Pallas kernels: 222 us -> 179 us
    pallas_call x1, Pallas kernels: 222 us -> 179 us  [fused_on_device(): pl.pallas_call(functools.partial(fused_kernel, n), out_shape=(jax.ShapeDt...]
where the time goes in v2:
time: 189 us
  Pallas kernels  179 us (95%)
  local copies, waits for them, and re-layouts  7.79 us (4%)
  between operations  1.93 us (1%)
    pallas_call x1, Pallas kernels, fused_on_device(): pl.pallas_call(functools.partial(fused_kernel, n), out_shape=(jax.ShapeDt...  179 us
    unnamed x2, local copies, waits for them, and re-layouts  6.53 us

profile of v2, /device:TPU:11, one launch (start us, length us, event | category | flops | bytes accessed | tf_op | source)
XLA Modules:
  0.0 189.0 jit_solution(1418730314709018289)
XLA Ops:
  1.9 1.3 broadcast_in_dim.3.alpha
  3.2 179.2 %snake_conv_fused.1 = (bf16[7,128,768]{2,1,0:T(8,128)(2,1)}, f32[3,384,768]{2,1,0:T(8,128)}) custom-call(bf16[12,128,768]{2,1,0:T(8,128)(2,1)} %feat.1, bf16[12,128,768]{2,1,0:T(8,128)(2,1)} %cot.1, f32[1,768]{1,0:T(1,128)} %broadcast_in_dim.3.alpha, bf16[3,384,768]{2,1,0:T(8,128)(2,1)} %bitcast.3, s32[12]{0:T(128)} %lengths.1, s32[1]{0:T(128)S(6)} %copy.11.kept, ...), custom_call_target="tpu_custom_call" | custom-call | flops 21743271936 | bytes 16777216 | tf_op jit(solution)/shard_map/snake_conv_fused/pallas_call | solution.py:466
  182.4 2.5 %copy.13 = bf16[7,128,768]{2,1,0:T(8,128)(2,1)} copy(bf16[7,128,768]{2,1,0:T(8,128)(2,1)} %get-tuple-element.8) | data formatting | bytes 2752512
  184.9 4.0 %copy.14 = f32[384,3,768]{2,0,1:T(8,128)} copy(f32[384,3,768]{2,0,1:T(8,128)} %bitcast.2) | data formatting | bytes 7077888
